TPU v7x, 32 devices: a whole 2x2x4 slice. The times are simulated.
32 devices in a mesh: rows: 4 (over z), segment: 4 (over y, x), tm: 2 (over core).
Axes of the slice: x: 2, y: 2, z: 4, core: 2. Of those that a mesh axis runs over, the one named last changes fastest.
Arguments:
- latents: bfloat16 [4, 8, 8, 128, 128], P(None, 'tm', 'rows'), may hold values from -40 to 40
- conv_first: bfloat16 [4, 3, 3, 3, 128, 128], P('segment'), may hold values from -0.109375 to 0.109375
- conv_second: bfloat16 [4, 3, 3, 3, 128, 128], P('segment'), may hold values from -0.109375 to 0.109375
- gain_first: bfloat16 [4, 128], P('segment'), may hold values from 0.099609375 to 1.8984375
- bias_first: bfloat16 [4, 128], P('segment'), may hold values from -1 to 1
- gain_second: bfloat16 [4, 128], P('segment'), may hold values from 0.099609375 to 1.8984375
- bias_second: bfloat16 [4, 128], P('segment'), may hold values from -1 to 1
Outputs:
- decoded: bfloat16 [4, 8, 8, 128, 128], P('segment', 'tm', 'rows')
All inputs are finite; a program needn't handle non-finite values.
Results may differ from a plain program's by a relative error of at most 0.022.
Values may be sent and summed in bfloat16 or wider, within the bound.
A program may use at most 64 MiB of HBM per device.

v0:
```python
import jax
import jax.numpy as jnp
from jax import lax
from jax.sharding import PartitionSpec as P

GROUPS = 32
EPS = 1e-06


def passed_along(value, axis, steps):
    count = lax.axis_size(axis)
    initial, last = (max(0, -steps), min(count, count - steps))
    return lax.ppermute(value, axis, [(source, source + steps) for source in range(initial, last)])


def padded_2(block, sides, width):
    for axis, dim in sides:
        count = lax.axis_size(axis)
        forward = [(i, i + 1) for i in range(count - 1)]
        backward = [(target, source) for source, target in forward]
        low = lax.ppermute(
            lax.slice_in_dim(block, block.shape[dim] - width, None, axis=dim), axis, forward
        )
        high = lax.ppermute(lax.slice_in_dim(block, 0, width, axis=dim), axis, backward)
        block = jnp.concatenate([low, block, high], axis=dim)
    return block


def normalize(values, norm_gain, norm_bias):
    frames, rows_here, columns, channels = values.shape
    width_group = channels // GROUPS
    grouped = values.astype(jnp.float32).reshape(frames, rows_here, columns, GROUPS, width_group)
    totals = lax.psum(
        (jnp.sum(grouped, axis=(0, 1, 2, 4)), jnp.sum(grouped * grouped, axis=(0, 1, 2, 4))), "rows"
    )
    members = frames * rows_here * lax.axis_size("rows") * columns * width_group
    average = totals[0] / members
    squares = totals[1] / members
    inverse = lax.rsqrt(squares - average * average + EPS)
    scaled = (grouped - average[:, None]) * inverse[:, None]
    scaled = scaled.reshape(values.shape) * norm_gain.astype(jnp.float32) + norm_bias.astype(
        jnp.float32
    )
    return jax.nn.silu(scaled).astype(jnp.bfloat16)


def convolve(active, kernel):
    previous = passed_along(active[-2:], "tm", 1)
    extended = jnp.concatenate([previous, active], axis=0)
    padded = padded_2(extended, (("rows", 1),), 1)
    padded = jnp.pad(padded, ((0, 0), (0, 0), (1, 1), (0, 0)))
    result = lax.conv_general_dilated(
        padded[None],
        kernel,
        (1, 1, 1),
        "VALID",
        dimension_numbers=("NDHWC", "DHWIO", "NDHWC"),
        preferred_element_type=jnp.float32,
    )
    return result[0]


def residual_block(values, params):
    first, second, gain_one, bias_one, gain_two, bias_two = params
    active = normalize(values, gain_one, bias_one)
    hidden = convolve(active, first).astype(jnp.bfloat16)
    active = normalize(hidden, gain_two, bias_two)
    return (values.astype(jnp.float32) + convolve(active, second)).astype(jnp.bfloat16)


def body(latents, conv_first, conv_second, gain_first, bias_first, gain_second, bias_second):
    segments = lax.axis_size("segment")
    micro = latents.shape[0]
    per_segment = micro // segments
    position = lax.axis_index("segment")
    small = jnp.stack([gain_first, bias_first, gain_second, bias_second], axis=1)
    small = lax.all_gather(small, "segment", axis=0, tiled=True)
    first = lax.all_gather(conv_first, "segment", axis=0, tiled=True)
    second = lax.all_gather(conv_second, "segment", axis=0, tiled=True)
    outs = []
    for index in range(per_segment):
        values = lax.dynamic_index_in_dim(
            latents, position * per_segment + index, 0, keepdims=False
        )
        for layer in range(first.shape[0]):
            gains = small[layer]
            values = residual_block(
                values, (first[layer], second[layer], gains[0], gains[1], gains[2], gains[3])
            )
        outs.append(values)
    return jnp.stack(outs)


def solution(mesh):
    in_specs = (
        P(None, "tm", "rows", None, None),
        P("segment", None, None, None, None, None),
        P("segment", None, None, None, None, None),
        P("segment", None),
        P("segment", None),
        P("segment", None),
        P("segment", None),
    )
    out_specs = P("segment", "tm", "rows", None, None)
    return jax.shard_map(body, mesh=mesh, in_specs=in_specs, out_specs=out_specs, check_vma=False)
```

profile of v0, /device:TPU:0, one launch (start us, length us, event | category | flops | bytes accessed | tf_op | source)
XLA Modules:
  0.0 296.4 jit_solution(6094731690513591556)
XLA Ops:
  8.6 13.5 %all-reduce.15 = (f32[32]{0:T(128)S(1)}, f32[32]{0:T(128)S(1)}) all-reduce(f32[32]{0:T(128)S(1)} %reduce_sum.195, f32[32]{0:T(128)S(1)} %reduce_sum.189), channel_id=1, replica_groups=mesh['rows'=4,'segment'=4,'tm'=2] {'rows'}, use_global_device_ids=true, to_apply=%region_5.6 | all-reduce | flops 64 | bytes 512 | tf_op jit(solution)/shard_map/psum | solution.py:33
  22.5 8.1 %all_gather.9 = bf16[4,4,128]{2,1,0:T(4,128)(2,1)S(1)} all-gather(bf16[1,4,128]{2,1,0:T(4,128)(2,1)S(1)} %pad_maximum_fusion.8), channel_id=1, replica_groups=mesh['rows'=4,'segment'=4,'tm'=2] {'segment'}, dimensions={0}, use_global_device_ids=true | all-gather | bytes 5120 | tf_op jit(solution)/shard_map/all_gather | solution.py:77
  30.9 1.3 collective-permute-start
  33.2 1.3 collective-permute-start.1
  35.8 3.6 %collective-permute-done.1 = bf16[6,1,128,128]{3,2,1,0:T(8,128)(2,1)S(1)} collective-permute-done((bf16[6,1,128,128]{3,2,1,0:T(8,128)(2,1)S(1)}, bf16[6,1,128,128]{3,2,1,0:T(8,128)(2,1)S(1)}, u32[]{:S(2)}, u32[]{:S(2)}) %collective-permute-start.1) | collective-permute-done | bytes 196640 | tf_op jit(solution)/shard_map/ppermute | solution.py:21
  39.4 4.1 %collective-permute-done.2 = bf16[6,1,128,128]{3,2,1,0:T(8,128)(2,1)S(1)} collective-permute-done((bf16[6,1,128,128]{3,2,1,0:T(8,128)(2,1)S(1)}, bf16[6,1,128,128]{3,2,1,0:T(8,128)(2,1)S(1)}, u32[]{:S(2)}, u32[]{:S(2)}) %collective-permute-start.2) | collective-permute-done | bytes 196640 | tf_op jit(solution)/shard_map/ppermute | solution.py:24
  44.6 14.6 %all-gather.3.cloned.1.call-done = bf16[4,3,3,3,128,128]{5,4,3,2,1,0:T(8,128)(2,1)} async-done(((bf16[1,3,3,3,128,128]{5,4,3,2,1,0:T(8,128)(2,1)}), bf16[4,3,3,3,128,128]{5,4,3,2,1,0:T(8,128)(2,1)}) %all-gather.3.cloned.1.call-update) | async-done | bytes 3538960 | tf_op jit(solution)/shard_map/all_gather | solution.py:78
  59.2 3.3 %fusion.81 = (f32[128]{0:T(128)S(1)}, f32[128]{0:T(128)S(1)}, bf16[4,2,8,17,128]{4,2,3,1,0:T(8,128)(2,1)S(1)}) fusion(pred[8,17]{0,1:T(8,128)(4,1)S(1)} %copy-done.5, bf16[4,3,3,3,128,128]{5,4,3,2,1,0:T(8,128)(2,1)} %all-gather.3.cloned.1.call-done, bf16[6,4,1,7,2,128]{5,3,4,1,0,2:T(8,128)(2,1)S(1)} %slice.249, bf16[6,4,1,8,17,128]{5,3,4,1,0,2:T(8,128)(2,1)S(1)} %copy.62), kind=kOutput, calls=%fused_computation.137 | convolution fusion | flops 966508288 | bytes 2086024 | tf_op jit(solution)/shard_map/conv_general_dilated | solution.py:52
  63.0 11.7 %all-reduce.14 = (f32[32]{0:T(128)S(1)}, f32[32]{0:T(128)S(1)}) all-reduce(f32[32]{0:T(128)S(1)} %reduce_sum.204, f32[32]{0:T(128)S(1)} %reduce_sum.201), channel_id=1, replica_groups=mesh['rows'=4,'segment'=4,'tm'=2] {'rows'}, use_global_device_ids=true, to_apply=%region_11.12 | all-reduce | flops 64 | bytes 512 | tf_op jit(solution)/shard_map/psum | solution.py:33
  78.0 1.3 collective-permute-start.4
  80.6 3.6 %collective-permute-done.4 = bf16[6,1,128,128]{3,2,1,0:T(8,128)(2,1)S(1)} collective-permute-done((bf16[6,1,128,128]{3,2,1,0:T(8,128)(2,1)S(1)}, bf16[6,1,128,128]{3,2,1,0:T(8,128)(2,1)S(1)}, u32[]{:S(2)}, u32[]{:S(2)}) %collective-permute-start.4) | collective-permute-done | bytes 196640 | tf_op jit(solution)/shard_map/ppermute | solution.py:21
  84.3 4.1 %collective-permute-done.5 = bf16[6,1,128,128]{3,2,1,0:T(8,128)(2,1)S(1)} collective-permute-done((bf16[6,1,128,128]{3,2,1,0:T(8,128)(2,1)S(1)}, bf16[6,1,128,128]{3,2,1,0:T(8,128)(2,1)S(1)}, u32[]{:S(2)}, u32[]{:S(2)}) %collective-permute-start.5) | collective-permute-done | bytes 196640 | tf_op jit(solution)/shard_map/ppermute | solution.py:24
  89.4 18.9 %all-gather.5.cloned.1.call-done = bf16[4,3,3,3,128,128]{5,4,3,2,1,0:T(8,128)(2,1)} async-done(((bf16[1,3,3,3,128,128]{5,4,3,2,1,0:T(8,128)(2,1)}), bf16[4,3,3,3,128,128]{5,4,3,2,1,0:T(8,128)(2,1)}) %all-gather.5.cloned.1.call-update) | async-done | bytes 3538960 | tf_op jit(solution)/shard_map/all_gather | solution.py:79
  108.4 3.3 %convolution_select_fusion.6 = f32[4,2,8,17,128]{4,2,3,1,0:T(8,128)S(1)} fusion(bf16[6,4,1,7,2,128]{5,3,4,1,0,2:T(8,128)(2,1)S(1)} %slice.257, bf16[6,4,1,8,17,128]{5,3,4,1,0,2:T(8,128)(2,1)S(1)} %copy.67, bf16[4,3,3,3,128,128]{5,4,3,2,1,0:T(8,128)(2,1)} %all-gather.5.cloned.1.call-done, pred[8,17]{0,1:T(8,128)(4,1)S(1)} %copy-done.5), kind=kOutput, calls=%fused_computation.18 | convolution fusion | flops 965533696 | bytes 2363528 | tf_op jit(solution)/shard_map/conv_general_dilated | solution.py:52
  112.6 11.7 %all-reduce.13 = (f32[32]{0:T(128)S(1)}, f32[32]{0:T(128)S(1)}) all-reduce(f32[32]{0:T(128)S(1)} %reduce_sum.216, f32[32]{0:T(128)S(1)} %reduce_sum.210), channel_id=1, replica_groups=mesh['rows'=4,'segment'=4,'tm'=2] {'rows'}, use_global_device_ids=true, to_apply=%region_17.18 | all-reduce | flops 64 | bytes 512 | tf_op jit(solution)/shard_map/psum | solution.py:33
  124.9 1.3 collective-permute-start.6
  127.3 1.3 collective-permute-start.7
  128.6 1.5 collective-permute-start.8
  130.0 3.5 %collective-permute-done.7 = bf16[6,1,128,128]{3,2,1,0:T(8,128)(2,1)S(1)} collective-permute-done((bf16[6,1,128,128]{3,2,1,0:T(8,128)(2,1)S(1)}, bf16[6,1,128,128]{3,2,1,0:T(8,128)(2,1)S(1)}, u32[]{:S(2)}, u32[]{:S(2)}) %collective-permute-start.7) | collective-permute-done | bytes 196640 | tf_op jit(solution)/shard_map/ppermute | solution.py:21
  133.5 4.1 %collective-permute-done.8 = bf16[6,1,128,128]{3,2,1,0:T(8,128)(2,1)S(1)} collective-permute-done((bf16[6,1,128,128]{3,2,1,0:T(8,128)(2,1)S(1)}, bf16[6,1,128,128]{3,2,1,0:T(8,128)(2,1)S(1)}, u32[]{:S(2)}, u32[]{:S(2)}) %collective-permute-start.8) | collective-permute-done | bytes 196640 | tf_op jit(solution)/shard_map/ppermute | solution.py:24
  138.7 3.3 %fusion.84 = (f32[128]{0:T(128)S(1)}, f32[128]{0:T(128)S(1)}, bf16[4,2,8,17,128]{4,2,3,1,0:T(8,128)(2,1)S(1)}) fusion(pred[8,17]{0,1:T(8,128)(4,1)S(1)} %copy-done.5, bf16[4,3,3,3,128,128]{5,4,3,2,1,0:T(8,128)(2,1)} %all-gather.3.cloned.1.call-done, bf16[6,4,1,7,2,128]{5,3,4,1,0,2:T(8,128)(2,1)S(1)} %slice.265, bf16[6,4,1,8,17,128]{5,3,4,1,0,2:T(8,128)(2,1)S(1)} %copy.72), kind=kOutput, calls=%fused_computation.140 | convolution fusion | flops 966508288 | bytes 2086024 | tf_op jit(solution)/shard_map/conv_general_dilated | solution.py:52
  142.5 8.9 %all-reduce.12 = (f32[32]{0:T(128)S(1)}, f32[32]{0:T(128)S(1)}) all-reduce(f32[32]{0:T(128)S(1)} %reduce_sum.225, f32[32]{0:T(128)S(1)} %reduce_sum.219), channel_id=1, replica_groups=mesh['rows'=4,'segment'=4,'tm'=2] {'rows'}, use_global_device_ids=true, to_apply=%region_23.24 | all-reduce | flops 64 | bytes 512 | tf_op jit(solution)/shard_map/psum | solution.py:33
  152.4 1.3 collective-permute-start.9
  154.7 3.4 %collective-permute-start.10 = (bf16[6,1,128,128]{3,2,1,0:T(8,128)(2,1)S(1)}, bf16[6,1,128,128]{3,2,1,0:T(8,128)(2,1)S(1)}, u32[]{:S(2)}, u32[]{:S(2)}) collective-permute-start(bf16[6,1,128,128]{3,2,1,0:T(8,128)(2,1)S(1)} %get-tuple-element.50), channel_id=1, source_target_pairs={{0,8},{8,16},{16,24},{1,9},{9,17},{17,25},{2,10},{10,18},{18,26},{... | collective-permute-start | bytes 589832 | tf_op jit(solution)/shard_map/ppermute | solution.py:21
  159.4 3.3 %collective-permute-done.10 = bf16[6,1,128,128]{3,2,1,0:T(8,128)(2,1)S(1)} collective-permute-done((bf16[6,1,128,128]{3,2,1,0:T(8,128)(2,1)S(1)}, bf16[6,1,128,128]{3,2,1,0:T(8,128)(2,1)S(1)}, u32[]{:S(2)}, u32[]{:S(2)}) %collective-permute-start.10) | collective-permute-done | bytes 196640 | tf_op jit(solution)/shard_map/ppermute | solution.py:21
  162.7 4.1 %collective-permute-done.11 = bf16[6,1,128,128]{3,2,1,0:T(8,128)(2,1)S(1)} collective-permute-done((bf16[6,1,128,128]{3,2,1,0:T(8,128)(2,1)S(1)}, bf16[6,1,128,128]{3,2,1,0:T(8,128)(2,1)S(1)}, u32[]{:S(2)}, u32[]{:S(2)}) %collective-permute-start.11) | collective-permute-done | bytes 196640 | tf_op jit(solution)/shard_map/ppermute | solution.py:24
  167.9 3.3 %convolution_select_fusion.4 = f32[4,2,8,17,128]{4,2,3,1,0:T(8,128)S(1)} fusion(bf16[6,4,1,7,2,128]{5,3,4,1,0,2:T(8,128)(2,1)S(1)} %slice.273, bf16[6,4,1,8,17,128]{5,3,4,1,0,2:T(8,128)(2,1)S(1)} %copy.77, bf16[4,3,3,3,128,128]{5,4,3,2,1,0:T(8,128)(2,1)} %all-gather.5.cloned.1.call-done, pred[8,17]{0,1:T(8,128)(4,1)S(1)} %copy-done.5), kind=kOutput, calls=%fused_computation.16 | convolution fusion | flops 965533696 | bytes 2363528 | tf_op jit(solution)/shard_map/conv_general_dilated | solution.py:52
  172.1 8.7 %all-reduce.11 = (f32[32]{0:T(128)S(1)}, f32[32]{0:T(128)S(1)}) all-reduce(f32[32]{0:T(128)S(1)} %reduce_sum.234, f32[32]{0:T(128)S(1)} %reduce_sum.231), channel_id=1, replica_groups=mesh['rows'=4,'segment'=4,'tm'=2] {'rows'}, use_global_device_ids=true, to_apply=%region_29.30 | all-reduce | flops 64 | bytes 512 | tf_op jit(solution)/shard_map/psum | solution.py:33
  183.7 3.6 %collective-permute-start.13 = (bf16[6,1,128,128]{3,2,1,0:T(8,128)(2,1)S(1)}, bf16[6,1,128,128]{3,2,1,0:T(8,128)(2,1)S(1)}, u32[]{:S(2)}, u32[]{:S(2)}) collective-permute-start(bf16[6,1,128,128]{3,2,1,0:T(8,128)(2,1)S(1)} %get-tuple-element.48), channel_id=1, source_target_pairs={{0,8},{8,16},{16,24},{1,9},{9,17},{17,25},{2,10},{10,18},{18,26},{... | collective-permute-start | bytes 589832 | tf_op jit(solution)/shard_map/ppermute | solution.py:21
  188.6 3.3 %collective-permute-done.13 = bf16[6,1,128,128]{3,2,1,0:T(8,128)(2,1)S(1)} collective-permute-done((bf16[6,1,128,128]{3,2,1,0:T(8,128)(2,1)S(1)}, bf16[6,1,128,128]{3,2,1,0:T(8,128)(2,1)S(1)}, u32[]{:S(2)}, u32[]{:S(2)}) %collective-permute-start.13) | collective-permute-done | bytes 196640 | tf_op jit(solution)/shard_map/ppermute | solution.py:21
  192.0 4.1 %collective-permute-done.14 = bf16[6,1,128,128]{3,2,1,0:T(8,128)(2,1)S(1)} collective-permute-done((bf16[6,1,128,128]{3,2,1,0:T(8,128)(2,1)S(1)}, bf16[6,1,128,128]{3,2,1,0:T(8,128)(2,1)S(1)}, u32[]{:S(2)}, u32[]{:S(2)}) %collective-permute-start.14) | collective-permute-done | bytes 196640 | tf_op jit(solution)/shard_map/ppermute | solution.py:24
  197.2 3.3 %fusion.87 = (f32[128]{0:T(128)S(1)}, f32[128]{0:T(128)S(1)}, bf16[4,2,8,17,128]{4,2,3,1,0:T(8,128)(2,1)S(1)}) fusion(pred[8,17]{0,1:T(8,128)(4,1)S(1)} %copy-done.5, bf16[4,3,3,3,128,128]{5,4,3,2,1,0:T(8,128)(2,1)} %all-gather.3.cloned.1.call-done, bf16[6,4,1,7,2,128]{5,3,4,1,0,2:T(8,128)(2,1)S(1)} %slice.281, bf16[6,4,1,8,17,128]{5,3,4,1,0,2:T(8,128)(2,1)S(1)} %copy.82), kind=kOutput, calls=%fused_computation.143 | convolution fusion | flops 966508288 | bytes 2086024 | tf_op jit(solution)/shard_map/conv_general_dilated | solution.py:52
  200.9 8.9 %all-reduce.10 = (f32[32]{0:T(128)S(1)}, f32[32]{0:T(128)S(1)}) all-reduce(f32[32]{0:T(128)S(1)} %reduce_sum.291, f32[32]{0:T(128)S(1)} %reduce_sum.288), channel_id=1, replica_groups=mesh['rows'=4,'segment'=4,'tm'=2] {'rows'}, use_global_device_ids=true, to_apply=%region_35.36 | all-reduce | flops 64 | bytes 512 | tf_op jit(solution)/shard_map/psum | solution.py:33
  213.1 3.6 %collective-permute-start.16 = (bf16[6,1,128,128]{3,2,1,0:T(8,128)(2,1)S(1)}, bf16[6,1,128,128]{3,2,1,0:T(8,128)(2,1)S(1)}, u32[]{:S(2)}, u32[]{:S(2)}) collective-permute-start(bf16[6,1,128,128]{3,2,1,0:T(8,128)(2,1)S(1)} %get-tuple-element.46), channel_id=1, source_target_pairs={{0,8},{8,16},{16,24},{1,9},{9,17},{17,25},{2,10},{10,18},{18,26},{... | collective-permute-start | bytes 589832 | tf_op jit(solution)/shard_map/ppermute | solution.py:21
  218.1 3.3 %collective-permute-done.16 = bf16[6,1,128,128]{3,2,1,0:T(8,128)(2,1)S(1)} collective-permute-done((bf16[6,1,128,128]{3,2,1,0:T(8,128)(2,1)S(1)}, bf16[6,1,128,128]{3,2,1,0:T(8,128)(2,1)S(1)}, u32[]{:S(2)}, u32[]{:S(2)}) %collective-permute-start.16) | collective-permute-done | bytes 196640 | tf_op jit(solution)/shard_map/ppermute | solution.py:21
  221.4 4.1 %collective-permute-done.17 = bf16[6,1,128,128]{3,2,1,0:T(8,128)(2,1)S(1)} collective-permute-done((bf16[6,1,128,128]{3,2,1,0:T(8,128)(2,1)S(1)}, bf16[6,1,128,128]{3,2,1,0:T(8,128)(2,1)S(1)}, u32[]{:S(2)}, u32[]{:S(2)}) %collective-permute-start.17) | collective-permute-done | bytes 196640 | tf_op jit(solution)/shard_map/ppermute | solution.py:24
  226.6 3.3 %convolution_select_fusion.2 = f32[4,2,8,17,128]{4,2,3,1,0:T(8,128)S(1)} fusion(bf16[6,4,1,7,2,128]{5,3,4,1,0,2:T(8,128)(2,1)S(1)} %slice.289, bf16[6,4,1,8,17,128]{5,3,4,1,0,2:T(8,128)(2,1)S(1)} %copy.87, bf16[4,3,3,3,128,128]{5,4,3,2,1,0:T(8,128)(2,1)} %all-gather.5.cloned.1.call-done, pred[8,17]{0,1:T(8,128)(4,1)S(1)} %copy-done.5), kind=kOutput, calls=%fused_computation.14 | convolution fusion | flops 965533696 | bytes 2363528 | tf_op jit(solution)/shard_map/conv_general_dilated | solution.py:52
  230.8 8.6 %all-reduce.9 = (f32[32]{0:T(128)S(1)}, f32[32]{0:T(128)S(1)}) all-reduce(f32[32]{0:T(128)S(1)} %reduce_sum.297, f32[32]{0:T(128)S(1)} %reduce_sum.294), channel_id=1, replica_groups=mesh['rows'=4,'segment'=4,'tm'=2] {'rows'}, use_global_device_ids=true, to_apply=%region_41.42 | all-reduce | flops 64 | bytes 512 | tf_op jit(solution)/shard_map/psum | solution.py:33
  242.4 3.6 %collective-permute-start.19 = (bf16[6,1,128,128]{3,2,1,0:T(8,128)(2,1)S(1)}, bf16[6,1,128,128]{3,2,1,0:T(8,128)(2,1)S(1)}, u32[]{:S(2)}, u32[]{:S(2)}) collective-permute-start(bf16[6,1,128,128]{3,2,1,0:T(8,128)(2,1)S(1)} %get-tuple-element.44), channel_id=1, source_target_pairs={{0,8},{8,16},{16,24},{1,9},{9,17},{17,25},{2,10},{10,18},{18,26},{... | collective-permute-start | bytes 589832 | tf_op jit(solution)/shard_map/ppermute | solution.py:21
  247.4 3.3 %collective-permute-done.19 = bf16[6,1,128,128]{3,2,1,0:T(8,128)(2,1)S(1)} collective-permute-done((bf16[6,1,128,128]{3,2,1,0:T(8,128)(2,1)S(1)}, bf16[6,1,128,128]{3,2,1,0:T(8,128)(2,1)S(1)}, u32[]{:S(2)}, u32[]{:S(2)}) %collective-permute-start.19) | collective-permute-done | bytes 196640 | tf_op jit(solution)/shard_map/ppermute | solution.py:21
  250.7 4.1 %collective-permute-done.20 = bf16[6,1,128,128]{3,2,1,0:T(8,128)(2,1)S(1)} collective-permute-done((bf16[6,1,128,128]{3,2,1,0:T(8,128)(2,1)S(1)}, bf16[6,1,128,128]{3,2,1,0:T(8,128)(2,1)S(1)}, u32[]{:S(2)}, u32[]{:S(2)}) %collective-permute-start.20) | collective-permute-done | bytes 196640 | tf_op jit(solution)/shard_map/ppermute | solution.py:24
  255.9 3.3 %fusion.90 = (f32[128]{0:T(128)S(1)}, f32[128]{0:T(128)S(1)}, bf16[4,2,8,17,128]{4,2,3,1,0:T(8,128)(2,1)S(1)}) fusion(pred[8,17]{0,1:T(8,128)(4,1)S(1)} %copy-done.5, bf16[4,3,3,3,128,128]{5,4,3,2,1,0:T(8,128)(2,1)} %all-gather.3.cloned.1.call-done, bf16[6,4,1,7,2,128]{5,3,4,1,0,2:T(8,128)(2,1)S(1)} %slice.297, bf16[6,4,1,8,17,128]{5,3,4,1,0,2:T(8,128)(2,1)S(1)} %copy.92), kind=kOutput, calls=%fused_computation.146 | convolution fusion | flops 966508288 | bytes 2086024 | tf_op jit(solution)/shard_map/conv_general_dilated | solution.py:52
  259.7 8.7 %all-reduce.8 = (f32[32]{0:T(128)S(1)}, f32[32]{0:T(128)S(1)}) all-reduce(f32[32]{0:T(128)S(1)} %reduce_sum.303, f32[32]{0:T(128)S(1)} %reduce_sum.300), channel_id=1, replica_groups=mesh['rows'=4,'segment'=4,'tm'=2] {'rows'}, use_global_device_ids=true, to_apply=%region_47.48 | all-reduce | flops 64 | bytes 512 | tf_op jit(solution)/shard_map/psum | solution.py:33
  271.7 3.6 %collective-permute-start.22 = (bf16[6,1,128,128]{3,2,1,0:T(8,128)(2,1)S(1)}, bf16[6,1,128,128]{3,2,1,0:T(8,128)(2,1)S(1)}, u32[]{:S(2)}, u32[]{:S(2)}) collective-permute-start(bf16[6,1,128,128]{3,2,1,0:T(8,128)(2,1)S(1)} %get-tuple-element.42), channel_id=1, source_target_pairs={{0,8},{8,16},{16,24},{1,9},{9,17},{17,25},{2,10},{10,18},{18,26},{... | collective-permute-start | bytes 589832 | tf_op jit(solution)/shard_map/ppermute | solution.py:21
  275.3 1.6 collective-permute-start.23
  276.8 3.1 %collective-permute-done.22 = bf16[6,1,128,128]{3,2,1,0:T(8,128)(2,1)S(1)} collective-permute-done((bf16[6,1,128,128]{3,2,1,0:T(8,128)(2,1)S(1)}, bf16[6,1,128,128]{3,2,1,0:T(8,128)(2,1)S(1)}, u32[]{:S(2)}, u32[]{:S(2)}) %collective-permute-start.22) | collective-permute-done | bytes 196640 | tf_op jit(solution)/shard_map/ppermute | solution.py:21
  279.9 4.1 %collective-permute-done.23 = bf16[6,1,128,128]{3,2,1,0:T(8,128)(2,1)S(1)} collective-permute-done((bf16[6,1,128,128]{3,2,1,0:T(8,128)(2,1)S(1)}, bf16[6,1,128,128]{3,2,1,0:T(8,128)(2,1)S(1)}, u32[]{:S(2)}, u32[]{:S(2)}) %collective-permute-start.23) | collective-permute-done | bytes 196640 | tf_op jit(solution)/shard_map/ppermute | solution.py:24
  285.1 3.3 %convolution_select_fusion = f32[4,2,8,17,128]{4,2,3,1,0:T(8,128)S(1)} fusion(bf16[6,4,1,7,2,128]{5,3,4,1,0,2:T(8,128)(2,1)S(1)} %slice.305, bf16[6,4,1,8,17,128]{5,3,4,1,0,2:T(8,128)(2,1)S(1)} %copy.97, bf16[4,3,3,3,128,128]{5,4,3,2,1,0:T(8,128)(2,1)} %all-gather.5.cloned.1.call-done, pred[8,17]{0,1:T(8,128)(4,1)S(1)} %copy-done.5), kind=kOutput, calls=%fused_computation.12 | convolution fusion | flops 965533696 | bytes 2363528 | tf_op jit(solution)/shard_map/conv_general_dilated | solution.py:52
  (194 shorter events, 44.3 us)
Async XLA Ops:
  6.5 1.5 copy-start
  6.5 15.9 %copy-start.1 = (bf16[1,128]{1,0:T(2,128)(2,1)S(1)}, bf16[1,128]{1,0:T(2,128)(2,1)}, u32[]{:S(2)}) copy-start(bf16[1,128]{1,0:T(2,128)(2,1)} %param.13) | copy-start | bytes 772
  6.5 16.0 %copy-start.2 = (bf16[1,128]{1,0:T(2,128)(2,1)S(1)}, bf16[1,128]{1,0:T(2,128)(2,1)}, u32[]{:S(2)}) copy-start(bf16[1,128]{1,0:T(2,128)(2,1)} %param.12) | copy-start | bytes 772
  6.5 16.0 %copy-start.3 = (bf16[1,128]{1,0:T(2,128)(2,1)S(1)}, bf16[1,128]{1,0:T(2,128)(2,1)}, u32[]{:S(2)}) copy-start(bf16[1,128]{1,0:T(2,128)(2,1)} %param.11) | copy-start | bytes 772
  6.5 16.0 %copy-start.4 = (bf16[1,128]{1,0:T(2,128)(2,1)S(1)}, bf16[1,128]{1,0:T(2,128)(2,1)}, u32[]{:S(2)}) copy-start(bf16[1,128]{1,0:T(2,128)(2,1)} %param.10) | copy-start | bytes 772
  6.5 52.7 %all-gather.3.cloned.1.call-start = ((), (), s32[]{:S(2)}) async-start(), calls=%async_computation | async-start | bytes 4423680 | tf_op jit(solution)/shard_map/all_gather | solution.py:78
  7.3 101.1 %all-gather.5.cloned.1.call-start = ((), (), s32[]{:S(2)}) async-start(), calls=%async_computation.1 | async-start | bytes 4423680 | tf_op jit(solution)/shard_map/all_gather | solution.py:79
  30.9 2.3 collective-permute-start
  33.2 6.2 %collective-permute-start.1 = (bf16[6,1,128,128]{3,2,1,0:T(8,128)(2,1)S(1)}, bf16[6,1,128,128]{3,2,1,0:T(8,128)(2,1)S(1)}, u32[]{:S(2)}, u32[]{:S(2)}) collective-permute-start(bf16[6,1,128,128]{3,2,1,0:T(8,128)(2,1)S(1)} %get-tuple-element.56), channel_id=1, source_target_pairs={{0,8},{8,16},{16,24},{1,9},{9,17},{17,25},{2,10},{10,18},{18,26},{... | collective-permute-start | bytes 589832 | tf_op jit(solution)/shard_map/ppermute | solution.py:21
  34.5 9.1 %collective-permute-start.2 = (bf16[6,1,128,128]{3,2,1,0:T(8,128)(2,1)S(1)}, bf16[6,1,128,128]{3,2,1,0:T(8,128)(2,1)S(1)}, u32[]{:S(2)}, u32[]{:S(2)}) collective-permute-start(bf16[6,1,128,128]{3,2,1,0:T(8,128)(2,1)S(1)} %get-tuple-element.57), channel_id=1, source_target_pairs={{8,0},{16,8},{24,16},{9,1},{17,9},{25,17},{10,2},{18,10},{26,18},{... | collective-permute-start | bytes 589832 | tf_op jit(solution)/shard_map/ppermute | solution.py:24
  44.1 15.1 %copy-start.5 = (pred[8,17]{0,1:T(8,128)(4,1)S(1)}, pred[8,17]{0,1:T(8,128)(4,1)}, u32[]{:S(2)}) copy-start(pred[8,17]{0,1:T(8,128)(4,1)} %constant.110) | copy-start | bytes 412
  75.7 2.3 collective-permute-start.3
  78.0 6.2 %collective-permute-start.4 = (bf16[6,1,128,128]{3,2,1,0:T(8,128)(2,1)S(1)}, bf16[6,1,128,128]{3,2,1,0:T(8,128)(2,1)S(1)}, u32[]{:S(2)}, u32[]{:S(2)}) collective-permute-start(bf16[6,1,128,128]{3,2,1,0:T(8,128)(2,1)S(1)} %get-tuple-element.54), channel_id=1, source_target_pairs={{0,8},{8,16},{16,24},{1,9},{9,17},{17,25},{2,10},{10,18},{18,26},{... | collective-permute-start | bytes 589832 | tf_op jit(solution)/shard_map/ppermute | solution.py:21
  79.3 9.1 %collective-permute-start.5 = (bf16[6,1,128,128]{3,2,1,0:T(8,128)(2,1)S(1)}, bf16[6,1,128,128]{3,2,1,0:T(8,128)(2,1)S(1)}, u32[]{:S(2)}, u32[]{:S(2)}) collective-permute-start(bf16[6,1,128,128]{3,2,1,0:T(8,128)(2,1)S(1)} %get-tuple-element.55), channel_id=1, source_target_pairs={{8,0},{16,8},{24,16},{9,1},{17,9},{25,17},{10,2},{18,10},{26,18},{... | collective-permute-start | bytes 589832 | tf_op jit(solution)/shard_map/ppermute | solution.py:24
  124.9 2.3 collective-permute-start.6
  127.3 6.2 %collective-permute-start.7 = (bf16[6,1,128,128]{3,2,1,0:T(8,128)(2,1)S(1)}, bf16[6,1,128,128]{3,2,1,0:T(8,128)(2,1)S(1)}, u32[]{:S(2)}, u32[]{:S(2)}) collective-permute-start(bf16[6,1,128,128]{3,2,1,0:T(8,128)(2,1)S(1)} %get-tuple-element.52), channel_id=1, source_target_pairs={{0,8},{8,16},{16,24},{1,9},{9,17},{17,25},{2,10},{10,18},{18,26},{... | collective-permute-start | bytes 589832 | tf_op jit(solution)/shard_map/ppermute | solution.py:21
  128.6 9.1 %collective-permute-start.8 = (bf16[6,1,128,128]{3,2,1,0:T(8,128)(2,1)S(1)}, bf16[6,1,128,128]{3,2,1,0:T(8,128)(2,1)S(1)}, u32[]{:S(2)}, u32[]{:S(2)}) collective-permute-start(bf16[6,1,128,128]{3,2,1,0:T(8,128)(2,1)S(1)} %get-tuple-element.53), channel_id=1, source_target_pairs={{8,0},{16,8},{24,16},{9,1},{17,9},{25,17},{10,2},{18,10},{26,18},{... | collective-permute-start | bytes 589832 | tf_op jit(solution)/shard_map/ppermute | solution.py:24
  152.4 2.3 collective-permute-start.9
  154.7 8.0 %collective-permute-start.10 = (bf16[6,1,128,128]{3,2,1,0:T(8,128)(2,1)S(1)}, bf16[6,1,128,128]{3,2,1,0:T(8,128)(2,1)S(1)}, u32[]{:S(2)}, u32[]{:S(2)}) collective-permute-start(bf16[6,1,128,128]{3,2,1,0:T(8,128)(2,1)S(1)} %get-tuple-element.50), channel_id=1, source_target_pairs={{0,8},{8,16},{16,24},{1,9},{9,17},{17,25},{2,10},{10,18},{18,26},{... | collective-permute-start | bytes 589832 | tf_op jit(solution)/shard_map/ppermute | solution.py:21
  158.1 8.8 %collective-permute-start.11 = (bf16[6,1,128,128]{3,2,1,0:T(8,128)(2,1)S(1)}, bf16[6,1,128,128]{3,2,1,0:T(8,128)(2,1)S(1)}, u32[]{:S(2)}, u32[]{:S(2)}) collective-permute-start(bf16[6,1,128,128]{3,2,1,0:T(8,128)(2,1)S(1)} %get-tuple-element.51), channel_id=1, source_target_pairs={{8,0},{16,8},{24,16},{9,1},{17,9},{25,17},{10,2},{18,10},{26,18},{... | collective-permute-start | bytes 589832 | tf_op jit(solution)/shard_map/ppermute | solution.py:24
  181.4 2.3 collective-permute-start.12
  183.7 8.3 %collective-permute-start.13 = (bf16[6,1,128,128]{3,2,1,0:T(8,128)(2,1)S(1)}, bf16[6,1,128,128]{3,2,1,0:T(8,128)(2,1)S(1)}, u32[]{:S(2)}, u32[]{:S(2)}) collective-permute-start(bf16[6,1,128,128]{3,2,1,0:T(8,128)(2,1)S(1)} %get-tuple-element.48), channel_id=1, source_target_pairs={{0,8},{8,16},{16,24},{1,9},{9,17},{17,25},{2,10},{10,18},{18,26},{... | collective-permute-start | bytes 589832 | tf_op jit(solution)/shard_map/ppermute | solution.py:21
  187.3 8.8 %collective-permute-start.14 = (bf16[6,1,128,128]{3,2,1,0:T(8,128)(2,1)S(1)}, bf16[6,1,128,128]{3,2,1,0:T(8,128)(2,1)S(1)}, u32[]{:S(2)}, u32[]{:S(2)}) collective-permute-start(bf16[6,1,128,128]{3,2,1,0:T(8,128)(2,1)S(1)} %get-tuple-element.49), channel_id=1, source_target_pairs={{8,0},{16,8},{24,16},{9,1},{17,9},{25,17},{10,2},{18,10},{26,18},{... | collective-permute-start | bytes 589832 | tf_op jit(solution)/shard_map/ppermute | solution.py:24
  210.8 2.3 collective-permute-start.15
  213.1 8.3 %collective-permute-start.16 = (bf16[6,1,128,128]{3,2,1,0:T(8,128)(2,1)S(1)}, bf16[6,1,128,128]{3,2,1,0:T(8,128)(2,1)S(1)}, u32[]{:S(2)}, u32[]{:S(2)}) collective-permute-start(bf16[6,1,128,128]{3,2,1,0:T(8,128)(2,1)S(1)} %get-tuple-element.46), channel_id=1, source_target_pairs={{0,8},{8,16},{16,24},{1,9},{9,17},{17,25},{2,10},{10,18},{18,26},{... | collective-permute-start | bytes 589832 | tf_op jit(solution)/shard_map/ppermute | solution.py:21
  216.8 8.8 %collective-permute-start.17 = (bf16[6,1,128,128]{3,2,1,0:T(8,128)(2,1)S(1)}, bf16[6,1,128,128]{3,2,1,0:T(8,128)(2,1)S(1)}, u32[]{:S(2)}, u32[]{:S(2)}) collective-permute-start(bf16[6,1,128,128]{3,2,1,0:T(8,128)(2,1)S(1)} %get-tuple-element.47), channel_id=1, source_target_pairs={{8,0},{16,8},{24,16},{9,1},{17,9},{25,17},{10,2},{18,10},{26,18},{... | collective-permute-start | bytes 589832 | tf_op jit(solution)/shard_map/ppermute | solution.py:24
  240.1 2.3 collective-permute-start.18
  242.4 8.3 %collective-permute-start.19 = (bf16[6,1,128,128]{3,2,1,0:T(8,128)(2,1)S(1)}, bf16[6,1,128,128]{3,2,1,0:T(8,128)(2,1)S(1)}, u32[]{:S(2)}, u32[]{:S(2)}) collective-permute-start(bf16[6,1,128,128]{3,2,1,0:T(8,128)(2,1)S(1)} %get-tuple-element.44), channel_id=1, source_target_pairs={{0,8},{8,16},{16,24},{1,9},{9,17},{17,25},{2,10},{10,18},{18,26},{... | collective-permute-start | bytes 589832 | tf_op jit(solution)/shard_map/ppermute | solution.py:21
  246.1 8.8 %collective-permute-start.20 = (bf16[6,1,128,128]{3,2,1,0:T(8,128)(2,1)S(1)}, bf16[6,1,128,128]{3,2,1,0:T(8,128)(2,1)S(1)}, u32[]{:S(2)}, u32[]{:S(2)}) collective-permute-start(bf16[6,1,128,128]{3,2,1,0:T(8,128)(2,1)S(1)} %get-tuple-element.45), channel_id=1, source_target_pairs={{8,0},{16,8},{24,16},{9,1},{17,9},{25,17},{10,2},{18,10},{26,18},{... | collective-permute-start | bytes 589832 | tf_op jit(solution)/shard_map/ppermute | solution.py:24
  269.4 2.3 collective-permute-start.21
  271.7 8.3 %collective-permute-start.22 = (bf16[6,1,128,128]{3,2,1,0:T(8,128)(2,1)S(1)}, bf16[6,1,128,128]{3,2,1,0:T(8,128)(2,1)S(1)}, u32[]{:S(2)}, u32[]{:S(2)}) collective-permute-start(bf16[6,1,128,128]{3,2,1,0:T(8,128)(2,1)S(1)} %get-tuple-element.42), channel_id=1, source_target_pairs={{0,8},{8,16},{16,24},{1,9},{9,17},{17,25},{2,10},{10,18},{18,26},{... | collective-permute-start | bytes 589832 | tf_op jit(solution)/shard_map/ppermute | solution.py:21
  275.3 8.8 %collective-permute-start.23 = (bf16[6,1,128,128]{3,2,1,0:T(8,128)(2,1)S(1)}, bf16[6,1,128,128]{3,2,1,0:T(8,128)(2,1)S(1)}, u32[]{:S(2)}, u32[]{:S(2)}) collective-permute-start(bf16[6,1,128,128]{3,2,1,0:T(8,128)(2,1)S(1)} %get-tuple-element.43), channel_id=1, source_target_pairs={{8,0},{16,8},{24,16},{9,1},{17,9},{25,17},{10,2},{18,10},{26,18},{... | collective-permute-start | bytes 589832 | tf_op jit(solution)/shard_map/ppermute | solution.py:24
Sparse Core Ops, SparseCore 0:
  9.2 49.9 all-gather.2
  61.1 47.2 all-gather.4
where the time goes:
time: 297 us; the launch traced here: 296 us
  waiting for transfers between devices  103 us (35%)
  blocking collectives  88.7 us (30%)
  starting transfers between devices  43 us (14%)
  matrix products  26.5 us (9%)
  between operations  14.5 us (5%)
  local copies, waits for them, and re-layouts  13.6 us (5%)
  other arithmetic  7.41 us (2%)
    psum x8, blocking collectives, normalize(): lax.psum((jnp.sum(grouped, axis=(0, 1, 2, 4)), jnp.sum(grouped * grouped,...  80.6 us
    ppermute x8, waiting for transfers between devices, padded_2(): lax.ppermute(lax.slice_in_dim(block, 0, width, axis=dim), axis, backward)  33 us
    ppermute x8, waiting for transfers between devices, padded_2(): lax.ppermute(lax.slice_in_dim(block, block.shape[dim] - width, None, axis...  27.2 us
    conv_general_dilated x8, matrix products, convolve(): lax.conv_general_dilated(padded[None], kernel, (1, 1, 1), 'VALID', dimens...  26.5 us
    ppermute x8, starting transfers between devices, padded_2(): lax.ppermute(lax.slice_in_dim(block, block.shape[dim] - width, None, axis...  21.7 us
    all_gather x1, waiting for transfers between devices, body(): second = lax.all_gather(conv_second, 'segment', axis=0, tiled=True)  18.9 us
    all_gather x1, waiting for transfers between devices, body(): first = lax.all_gather(conv_first, 'segment', axis=0, tiled=True)  14.6 us
    ppermute x8, starting transfers between devices, padded_2(): lax.ppermute(lax.slice_in_dim(block, 0, width, axis=dim), axis, backward)  10.8 us
  transfers between devices with their start and end apart: 26, of which 26 were waited for; matrix products, arithmetic and copies ran while one was open for 3% of the time, Pallas kernels for 0%

commit v1 on v0

--- a/solution.py
+++ b/solution.py
@@ -76,7 +76,14 @@
     small = jnp.stack([gain_first, bias_first, gain_second, bias_second], axis=1)
     small = lax.all_gather(small, "segment", axis=0, tiled=True)
     first = lax.all_gather(conv_first, "segment", axis=0, tiled=True)
-    second = lax.all_gather(conv_second, "segment", axis=0, tiled=True)
+    ring = [conv_second]
+    for hop in range(3):
+        ring.append(lax.ppermute(ring[-1], "segment", [(dev, (dev + 1) % 4) for dev in range(4)]))
+    second = jnp.roll(
+        jnp.concatenate(ring[::-1], axis=0),
+        (lax.axis_index("segment") + 1) * ring[0].shape[0],
+        axis=0,
+    )
     outs = []
     for index in range(per_segment):
         values = lax.dynamic_index_in_dim(

time: 297 us -> 325 us (1.094)
  starting transfers between devices: 43 us -> 55.8 us
  local copies, waits for them, and re-layouts: 13.6 us -> 23.3 us
  blocking collectives: 88.7 us -> 97.6 us
  waiting for transfers between devices: 103 us -> 94.3 us
  other arithmetic: 7.41 us -> 11.3 us
    ppermute x0 -> x3, waiting for transfers between devices: none -> 29.4 us  [body(): lax.ppermute(ring[-1], 'segment', [(dev, (dev + 1) % 4) for dev in range(...]
    all_gather x1 -> x0, waiting for transfers between devices: 18.9 us -> none  [body(): second = lax.all_gather(conv_second, 'segment', axis=0, tiled=True)]
    all_gather x1, blocking collectives: 8.08 us -> 23.3 us  [body(): small = lax.all_gather(small, 'segment', axis=0, tiled=True)]
    all_gather x1, waiting for transfers between devices: 14.6 us -> 0.01 us  [body(): first = lax.all_gather(conv_first, 'segment', axis=0, tiled=True)]
    unnamed x20 -> x43, local copies, waits for them, and re-layouts: 2.5 us -> 10.5 us
    ppermute x0 -> x3, starting transfers between devices: none -> 6.83 us  [body(): lax.ppermute(ring[-1], 'segment', [(dev, (dev + 1) % 4) for dev in range(...]
    psum x8, blocking collectives: 80.6 us -> 74.3 us  [normalize(): lax.psum((jnp.sum(grouped, axis=(0, 1, 2, 4)), jnp.sum(grouped * grouped,...]
    ppermute x8, starting transfers between devices: 21.7 us -> 27.8 us  [padded_2(): lax.ppermute(lax.slice_in_dim(block, block.shape[dim] - width, None, axis...]
  transfers between devices with their start and end apart: 26 -> 28, of which waited for: 26 -> 24; matrix products, arithmetic and copies ran while one was open for 3% -> 5% of each run, Pallas kernels for 0% -> 0%
where the time goes in v1:
time: 325 us; the launch traced here: 324 us
  blocking collectives  97.6 us (30%)
  waiting for transfers between devices  94.3 us (29%)
  starting transfers between devices  55.8 us (17%)
  matrix products  26.7 us (8%)
  local copies, waits for them, and re-layouts  23.3 us (7%)
  between operations  14.6 us (4%)
  other arithmetic  11.3 us (3%)
    psum x8, blocking collectives, normalize(): lax.psum((jnp.sum(grouped, axis=(0, 1, 2, 4)), jnp.sum(grouped * grouped,...  74.3 us
    ppermute x8, waiting for transfers between devices, padded_2(): lax.ppermute(lax.slice_in_dim(block, 0, width, axis=dim), axis, backward)  32.9 us
    ppermute x3, waiting for transfers between devices, body(): lax.ppermute(ring[-1], 'segment', [(dev, (dev + 1) % 4) for dev in range(...  29.4 us
    ppermute x8, starting transfers between devices, padded_2(): lax.ppermute(lax.slice_in_dim(block, block.shape[dim] - width, None, axis...  27.8 us
    conv_general_dilated x8, matrix products, convolve(): lax.conv_general_dilated(padded[None], kernel, (1, 1, 1), 'VALID', dimens...  26.7 us
    ppermute x8, waiting for transfers between devices, padded_2(): lax.ppermute(lax.slice_in_dim(block, block.shape[dim] - width, None, axis...  24.6 us
    all_gather x1, blocking collectives, body(): small = lax.all_gather(small, 'segment', axis=0, tiled=True)  23.3 us
    ppermute x8, starting transfers between devices, padded_2(): lax.ppermute(lax.slice_in_dim(block, 0, width, axis=dim), axis, backward)  10.8 us
  transfers between devices with their start and end apart: 28, of which 24 were waited for; matrix products, arithmetic and copies ran while one was open for 5% of the time, Pallas kernels for 0%

profile of v1, /device:TPU:0, one launch (start us, length us, event | category | flops | bytes accessed | tf_op | source)
XLA Modules:
  0.0 323.7 jit_solution(7942882812171665199)
XLA Ops:
  7.3 3.0 collective-permute-start.6
  10.2 29.4 %collective-permute-done.6 = bf16[1,3,3,3,128,128]{5,4,3,2,1,0:T(8,128)(2,1)S(1)} collective-permute-done((bf16[1,3,3,3,128,128]{5,4,3,2,1,0:T(8,128)(2,1)}, bf16[1,3,3,3,128,128]{5,4,3,2,1,0:T(8,128)(2,1)S(1)}, u32[]{:S(2)}, u32[]{:S(2)}) %collective-permute-start.6) | collective-permute-done | bytes 884768 | tf_op jit(solution)/shard_map/ppermute | solution.py:81
  39.6 1.7 collective-permute-start.7
  42.9 12.0 %all-reduce.15 = (f32[32]{0:T(128)S(1)}, f32[32]{0:T(128)S(1)}) all-reduce(f32[32]{0:T(128)S(1)} %reduce_sum.195, f32[32]{0:T(128)S(1)} %reduce_sum.189), channel_id=1, replica_groups=mesh['rows'=4,'segment'=4,'tm'=2] {'rows'}, use_global_device_ids=true, to_apply=%region_5.6 | all-reduce | flops 64 | bytes 512 | tf_op jit(solution)/shard_map/psum | solution.py:33
  55.6 23.3 %all_gather.6 = bf16[4,4,128]{2,1,0:T(4,128)(2,1)S(1)} all-gather(bf16[1,4,128]{2,1,0:T(4,128)(2,1)S(1)} %pad_maximum_fusion.8), channel_id=1, replica_groups=mesh['rows'=4,'segment'=4,'tm'=2] {'segment'}, dimensions={0}, use_global_device_ids=true | all-gather | bytes 5120 | tf_op jit(solution)/shard_map/all_gather | solution.py:77
  79.5 2.1 collective-permute-start.8
  83.2 1.3 collective-permute-start
  86.2 3.6 %collective-permute-start.1 = (bf16[6,1,128,128]{3,2,1,0:T(8,128)(2,1)}, bf16[6,1,128,128]{3,2,1,0:T(8,128)(2,1)S(1)}, u32[]{:S(2)}, u32[]{:S(2)}) collective-permute-start(bf16[6,1,128,128]{3,2,1,0:T(8,128)(2,1)} %get-tuple-element.56), channel_id=1, source_target_pairs={{0,8},{8,16},{16,24},{1,9},{9,17},{17,25},{2,10},{10,18},{18,26},{... | collective-permute-start | bytes 589832 | tf_op jit(solution)/shard_map/ppermute | solution.py:21
  91.2 3.6 %collective-permute-done.1 = bf16[6,1,128,128]{3,2,1,0:T(8,128)(2,1)S(1)} collective-permute-done((bf16[6,1,128,128]{3,2,1,0:T(8,128)(2,1)}, bf16[6,1,128,128]{3,2,1,0:T(8,128)(2,1)S(1)}, u32[]{:S(2)}, u32[]{:S(2)}) %collective-permute-start.1) | collective-permute-done | bytes 196640 | tf_op jit(solution)/shard_map/ppermute | solution.py:21
  94.8 4.0 %collective-permute-done.2 = bf16[6,1,128,128]{3,2,1,0:T(8,128)(2,1)S(1)} collective-permute-done((bf16[6,1,128,128]{3,2,1,0:T(8,128)(2,1)}, bf16[6,1,128,128]{3,2,1,0:T(8,128)(2,1)S(1)}, u32[]{:S(2)}, u32[]{:S(2)}) %collective-permute-start.2) | collective-permute-done | bytes 196640 | tf_op jit(solution)/shard_map/ppermute | solution.py:24
  105.6 3.6 %fusion.81 = (f32[128]{0:T(128)S(1)}, f32[128]{0:T(128)S(1)}, bf16[4,2,8,17,128]{4,2,3,1,0:T(8,128)(2,1)S(1)}) fusion(pred[8,17]{0,1:T(8,128)(4,1)} %constant.132, bf16[4,3,3,3,128,128]{5,4,3,2,1,0:T(8,128)(2,1)} %all-gather.2.cloned.1.call-done, bf16[6,4,1,7,2,128]{5,3,4,1,0,2:T(8,128)(2,1)} %slice.249, bf16[6,4,1,8,17,128]{5,3,4,1,0,2:T(8,128)(2,1)} %copy-done.2), kind=kOutput, calls=%fused_computation.137 | convolution fusion | flops 966508288 | bytes 2101248 | tf_op jit(solution)/shard_map/conv_general_dilated | solution.py:52
  109.6 10.2 %all-reduce.14 = (f32[32]{0:T(128)S(1)}, f32[32]{0:T(128)S(1)}) all-reduce(f32[32]{0:T(128)S(1)} %reduce_sum.204, f32[32]{0:T(128)S(1)} %reduce_sum.201), channel_id=1, replica_groups=mesh['rows'=4,'segment'=4,'tm'=2] {'rows'}, use_global_device_ids=true, to_apply=%region_11.12 | all-reduce | flops 64 | bytes 512 | tf_op jit(solution)/shard_map/psum | solution.py:33
  123.3 2.4 collective-permute-start.4
  129.0 1.4 collective-permute-done.4
  130.3 4.1 %collective-permute-done.5 = bf16[6,1,128,128]{3,2,1,0:T(8,128)(2,1)S(1)} collective-permute-done((bf16[6,1,128,128]{3,2,1,0:T(8,128)(2,1)S(1)}, bf16[6,1,128,128]{3,2,1,0:T(8,128)(2,1)S(1)}, u32[]{:S(2)}, u32[]{:S(2)}) %collective-permute-start.5) | collective-permute-done | bytes 196640 | tf_op jit(solution)/shard_map/ppermute | solution.py:24
  135.7 3.3 %convolution_select_fusion.6 = f32[4,2,8,17,128]{4,2,3,1,0:T(8,128)S(1)} fusion(bf16[6,4,1,7,2,128]{5,3,4,1,0,2:T(8,128)(2,1)S(1)} %slice.257, bf16[6,4,1,8,17,128]{5,3,4,1,0,2:T(8,128)(2,1)S(1)} %copy.67, bf16[8,3,3,3,128,128]{5,4,3,2,1,0:T(8,128)(2,1)} %constant_dynamic-update-slice_fusion, s32[]{:T(128)S(6)} %select_n.19, pred[8,17]{0,1:T(8,128)(4,1)S(1)} %copy-done.13), kind=kOutput, calls=%fused_computation.18 | convolution fusion | flops 965533696 | bytes 2363532 | tf_op jit(solution)/shard_map/conv_general_dilated | solution.py:52
  140.8 8.7 %all-reduce.13 = (f32[32]{0:T(128)S(1)}, f32[32]{0:T(128)S(1)}) all-reduce(f32[32]{0:T(128)S(1)} %reduce_sum.216, f32[32]{0:T(128)S(1)} %reduce_sum.210), channel_id=1, replica_groups=mesh['rows'=4,'segment'=4,'tm'=2] {'rows'}, use_global_device_ids=true, to_apply=%region_17.18 | all-reduce | flops 64 | bytes 512 | tf_op jit(solution)/shard_map/psum | solution.py:33
  152.5 3.6 %collective-permute-start.10 = (bf16[6,1,128,128]{3,2,1,0:T(8,128)(2,1)S(1)}, bf16[6,1,128,128]{3,2,1,0:T(8,128)(2,1)S(1)}, u32[]{:S(2)}, u32[]{:S(2)}) collective-permute-start(bf16[6,1,128,128]{3,2,1,0:T(8,128)(2,1)S(1)} %get-tuple-element.52), channel_id=1, source_target_pairs={{0,8},{8,16},{16,24},{1,9},{9,17},{17,25},{2,10},{10,18},{18,26},{... | collective-permute-start | bytes 589832 | tf_op jit(solution)/shard_map/ppermute | solution.py:21
  156.1 1.5 collective-permute-start.11
  157.6 3.2 collective-permute-done.10
  160.7 4.1 %collective-permute-done.11 = bf16[6,1,128,128]{3,2,1,0:T(8,128)(2,1)S(1)} collective-permute-done((bf16[6,1,128,128]{3,2,1,0:T(8,128)(2,1)S(1)}, bf16[6,1,128,128]{3,2,1,0:T(8,128)(2,1)S(1)}, u32[]{:S(2)}, u32[]{:S(2)}) %collective-permute-start.11) | collective-permute-done | bytes 196640 | tf_op jit(solution)/shard_map/ppermute | solution.py:24
  165.9 3.3 %fusion.84 = (f32[128]{0:T(128)S(1)}, f32[128]{0:T(128)S(1)}, bf16[4,2,8,17,128]{4,2,3,1,0:T(8,128)(2,1)S(1)}) fusion(pred[8,17]{0,1:T(8,128)(4,1)S(1)} %copy-done.13, bf16[4,3,3,3,128,128]{5,4,3,2,1,0:T(8,128)(2,1)} %all-gather.2.cloned.1.call-done, bf16[6,4,1,7,2,128]{5,3,4,1,0,2:T(8,128)(2,1)S(1)} %slice.264, bf16[6,4,1,8,17,128]{5,3,4,1,0,2:T(8,128)(2,1)S(1)} %copy.72), kind=kOutput, calls=%fused_computation.140 | convolution fusion | flops 966508288 | bytes 2086024 | tf_op jit(solution)/shard_map/conv_general_dilated | solution.py:52
  169.7 8.7 %all-reduce.12 = (f32[32]{0:T(128)S(1)}, f32[32]{0:T(128)S(1)}) all-reduce(f32[32]{0:T(128)S(1)} %reduce_sum.225, f32[32]{0:T(128)S(1)} %reduce_sum.219), channel_id=1, replica_groups=mesh['rows'=4,'segment'=4,'tm'=2] {'rows'}, use_global_device_ids=true, to_apply=%region_23.24 | all-reduce | flops 64 | bytes 512 | tf_op jit(solution)/shard_map/psum | solution.py:33
  181.7 3.6 %collective-permute-start.13 = (bf16[6,1,128,128]{3,2,1,0:T(8,128)(2,1)S(1)}, bf16[6,1,128,128]{3,2,1,0:T(8,128)(2,1)S(1)}, u32[]{:S(2)}, u32[]{:S(2)}) collective-permute-start(bf16[6,1,128,128]{3,2,1,0:T(8,128)(2,1)S(1)} %get-tuple-element.50), channel_id=1, source_target_pairs={{0,8},{8,16},{16,24},{1,9},{9,17},{17,25},{2,10},{10,18},{18,26},{... | collective-permute-start | bytes 589832 | tf_op jit(solution)/shard_map/ppermute | solution.py:21
  186.6 3.3 %collective-permute-done.13 = bf16[6,1,128,128]{3,2,1,0:T(8,128)(2,1)S(1)} collective-permute-done((bf16[6,1,128,128]{3,2,1,0:T(8,128)(2,1)S(1)}, bf16[6,1,128,128]{3,2,1,0:T(8,128)(2,1)S(1)}, u32[]{:S(2)}, u32[]{:S(2)}) %collective-permute-start.13) | collective-permute-done | bytes 196640 | tf_op jit(solution)/shard_map/ppermute | solution.py:21
  190.0 4.1 %collective-permute-done.14 = bf16[6,1,128,128]{3,2,1,0:T(8,128)(2,1)S(1)} collective-permute-done((bf16[6,1,128,128]{3,2,1,0:T(8,128)(2,1)S(1)}, bf16[6,1,128,128]{3,2,1,0:T(8,128)(2,1)S(1)}, u32[]{:S(2)}, u32[]{:S(2)}) %collective-permute-start.14) | collective-permute-done | bytes 196640 | tf_op jit(solution)/shard_map/ppermute | solution.py:24
  195.2 3.3 %convolution_select_fusion.4 = f32[4,2,8,17,128]{4,2,3,1,0:T(8,128)S(1)} fusion(bf16[6,4,1,7,2,128]{5,3,4,1,0,2:T(8,128)(2,1)S(1)} %slice.272, bf16[6,4,1,8,17,128]{5,3,4,1,0,2:T(8,128)(2,1)S(1)} %copy.77, bf16[8,3,3,3,128,128]{5,4,3,2,1,0:T(8,128)(2,1)} %constant_dynamic-update-slice_fusion, s32[]{:T(128)S(6)} %add.267, pred[8,17]{0,1:T(8,128)(4,1)S(1)} %copy-done.13), kind=kOutput, calls=%fused_computation.16 | convolution fusion | flops 965533696 | bytes 2363532 | tf_op jit(solution)/shard_map/conv_general_dilated | solution.py:52
  199.4 8.7 %all-reduce.11 = (f32[32]{0:T(128)S(1)}, f32[32]{0:T(128)S(1)}) all-reduce(f32[32]{0:T(128)S(1)} %reduce_sum.234, f32[32]{0:T(128)S(1)} %reduce_sum.231), channel_id=1, replica_groups=mesh['rows'=4,'segment'=4,'tm'=2] {'rows'}, use_global_device_ids=true, to_apply=%region_29.30 | all-reduce | flops 64 | bytes 512 | tf_op jit(solution)/shard_map/psum | solution.py:33
  211.0 3.6 %collective-permute-start.16 = (bf16[6,1,128,128]{3,2,1,0:T(8,128)(2,1)S(1)}, bf16[6,1,128,128]{3,2,1,0:T(8,128)(2,1)S(1)}, u32[]{:S(2)}, u32[]{:S(2)}) collective-permute-start(bf16[6,1,128,128]{3,2,1,0:T(8,128)(2,1)S(1)} %get-tuple-element.48), channel_id=1, source_target_pairs={{0,8},{8,16},{16,24},{1,9},{9,17},{17,25},{2,10},{10,18},{18,26},{... | collective-permute-start | bytes 589832 | tf_op jit(solution)/shard_map/ppermute | solution.py:21
  215.9 3.3 %collective-permute-done.16 = bf16[6,1,128,128]{3,2,1,0:T(8,128)(2,1)S(1)} collective-permute-done((bf16[6,1,128,128]{3,2,1,0:T(8,128)(2,1)S(1)}, bf16[6,1,128,128]{3,2,1,0:T(8,128)(2,1)S(1)}, u32[]{:S(2)}, u32[]{:S(2)}) %collective-permute-start.16) | collective-permute-done | bytes 196640 | tf_op jit(solution)/shard_map/ppermute | solution.py:21
  219.3 4.1 %collective-permute-done.17 = bf16[6,1,128,128]{3,2,1,0:T(8,128)(2,1)S(1)} collective-permute-done((bf16[6,1,128,128]{3,2,1,0:T(8,128)(2,1)S(1)}, bf16[6,1,128,128]{3,2,1,0:T(8,128)(2,1)S(1)}, u32[]{:S(2)}, u32[]{:S(2)}) %collective-permute-start.17) | collective-permute-done | bytes 196640 | tf_op jit(solution)/shard_map/ppermute | solution.py:24
  224.5 3.3 %fusion.87 = (f32[128]{0:T(128)S(1)}, f32[128]{0:T(128)S(1)}, bf16[4,2,8,17,128]{4,2,3,1,0:T(8,128)(2,1)S(1)}) fusion(pred[8,17]{0,1:T(8,128)(4,1)S(1)} %copy-done.13, bf16[4,3,3,3,128,128]{5,4,3,2,1,0:T(8,128)(2,1)} %all-gather.2.cloned.1.call-done, bf16[6,4,1,7,2,128]{5,3,4,1,0,2:T(8,128)(2,1)S(1)} %slice.279, bf16[6,4,1,8,17,128]{5,3,4,1,0,2:T(8,128)(2,1)S(1)} %copy.82), kind=kOutput, calls=%fused_computation.143 | convolution fusion | flops 966508288 | bytes 2086024 | tf_op jit(solution)/shard_map/conv_general_dilated | solution.py:52
  228.2 8.9 %all-reduce.10 = (f32[32]{0:T(128)S(1)}, f32[32]{0:T(128)S(1)}) all-reduce(f32[32]{0:T(128)S(1)} %reduce_sum.291, f32[32]{0:T(128)S(1)} %reduce_sum.288), channel_id=1, replica_groups=mesh['rows'=4,'segment'=4,'tm'=2] {'rows'}, use_global_device_ids=true, to_apply=%region_35.36 | all-reduce | flops 64 | bytes 512 | tf_op jit(solution)/shard_map/psum | solution.py:33
  240.5 3.6 %collective-permute-start.19 = (bf16[6,1,128,128]{3,2,1,0:T(8,128)(2,1)S(1)}, bf16[6,1,128,128]{3,2,1,0:T(8,128)(2,1)S(1)}, u32[]{:S(2)}, u32[]{:S(2)}) collective-permute-start(bf16[6,1,128,128]{3,2,1,0:T(8,128)(2,1)S(1)} %get-tuple-element.46), channel_id=1, source_target_pairs={{0,8},{8,16},{16,24},{1,9},{9,17},{17,25},{2,10},{10,18},{18,26},{... | collective-permute-start | bytes 589832 | tf_op jit(solution)/shard_map/ppermute | solution.py:21
  245.4 3.3 %collective-permute-done.19 = bf16[6,1,128,128]{3,2,1,0:T(8,128)(2,1)S(1)} collective-permute-done((bf16[6,1,128,128]{3,2,1,0:T(8,128)(2,1)S(1)}, bf16[6,1,128,128]{3,2,1,0:T(8,128)(2,1)S(1)}, u32[]{:S(2)}, u32[]{:S(2)}) %collective-permute-start.19) | collective-permute-done | bytes 196640 | tf_op jit(solution)/shard_map/ppermute | solution.py:21
  248.7 4.1 %collective-permute-done.20 = bf16[6,1,128,128]{3,2,1,0:T(8,128)(2,1)S(1)} collective-permute-done((bf16[6,1,128,128]{3,2,1,0:T(8,128)(2,1)S(1)}, bf16[6,1,128,128]{3,2,1,0:T(8,128)(2,1)S(1)}, u32[]{:S(2)}, u32[]{:S(2)}) %collective-permute-start.20) | collective-permute-done | bytes 196640 | tf_op jit(solution)/shard_map/ppermute | solution.py:24
  253.9 3.3 %convolution_select_fusion.2 = f32[4,2,8,17,128]{4,2,3,1,0:T(8,128)S(1)} fusion(bf16[6,4,1,7,2,128]{5,3,4,1,0,2:T(8,128)(2,1)S(1)} %slice.287, bf16[6,4,1,8,17,128]{5,3,4,1,0,2:T(8,128)(2,1)S(1)} %copy.87, bf16[8,3,3,3,128,128]{5,4,3,2,1,0:T(8,128)(2,1)} %constant_dynamic-update-slice_fusion, s32[]{:T(128)S(6)} %add.268, pred[8,17]{0,1:T(8,128)(4,1)S(1)} %copy-done.13), kind=kOutput, calls=%fused_computation.14 | convolution fusion | flops 965533696 | bytes 2363532 | tf_op jit(solution)/shard_map/conv_general_dilated | solution.py:52
  258.2 8.7 %all-reduce.9 = (f32[32]{0:T(128)S(1)}, f32[32]{0:T(128)S(1)}) all-reduce(f32[32]{0:T(128)S(1)} %reduce_sum.297, f32[32]{0:T(128)S(1)} %reduce_sum.294), channel_id=1, replica_groups=mesh['rows'=4,'segment'=4,'tm'=2] {'rows'}, use_global_device_ids=true, to_apply=%region_41.42 | all-reduce | flops 64 | bytes 512 | tf_op jit(solution)/shard_map/psum | solution.py:33
  269.8 3.6 %collective-permute-start.22 = (bf16[6,1,128,128]{3,2,1,0:T(8,128)(2,1)S(1)}, bf16[6,1,128,128]{3,2,1,0:T(8,128)(2,1)S(1)}, u32[]{:S(2)}, u32[]{:S(2)}) collective-permute-start(bf16[6,1,128,128]{3,2,1,0:T(8,128)(2,1)S(1)} %get-tuple-element.44), channel_id=1, source_target_pairs={{0,8},{8,16},{16,24},{1,9},{9,17},{17,25},{2,10},{10,18},{18,26},{... | collective-permute-start | bytes 589832 | tf_op jit(solution)/shard_map/ppermute | solution.py:21
  274.7 3.3 %collective-permute-done.22 = bf16[6,1,128,128]{3,2,1,0:T(8,128)(2,1)S(1)} collective-permute-done((bf16[6,1,128,128]{3,2,1,0:T(8,128)(2,1)S(1)}, bf16[6,1,128,128]{3,2,1,0:T(8,128)(2,1)S(1)}, u32[]{:S(2)}, u32[]{:S(2)}) %collective-permute-start.22) | collective-permute-done | bytes 196640 | tf_op jit(solution)/shard_map/ppermute | solution.py:21
  278.0 4.1 %collective-permute-done.23 = bf16[6,1,128,128]{3,2,1,0:T(8,128)(2,1)S(1)} collective-permute-done((bf16[6,1,128,128]{3,2,1,0:T(8,128)(2,1)S(1)}, bf16[6,1,128,128]{3,2,1,0:T(8,128)(2,1)S(1)}, u32[]{:S(2)}, u32[]{:S(2)}) %collective-permute-start.23) | collective-permute-done | bytes 196640 | tf_op jit(solution)/shard_map/ppermute | solution.py:24
  283.2 3.3 %fusion.90 = (f32[128]{0:T(128)S(1)}, f32[128]{0:T(128)S(1)}, bf16[4,2,8,17,128]{4,2,3,1,0:T(8,128)(2,1)S(1)}) fusion(pred[8,17]{0,1:T(8,128)(4,1)S(1)} %copy-done.13, bf16[4,3,3,3,128,128]{5,4,3,2,1,0:T(8,128)(2,1)} %all-gather.2.cloned.1.call-done, bf16[6,4,1,7,2,128]{5,3,4,1,0,2:T(8,128)(2,1)S(1)} %slice.294, bf16[6,4,1,8,17,128]{5,3,4,1,0,2:T(8,128)(2,1)S(1)} %copy.92), kind=kOutput, calls=%fused_computation.146 | convolution fusion | flops 966508288 | bytes 2086024 | tf_op jit(solution)/shard_map/conv_general_dilated | solution.py:52
  287.0 8.7 %all-reduce.8 = (f32[32]{0:T(128)S(1)}, f32[32]{0:T(128)S(1)}) all-reduce(f32[32]{0:T(128)S(1)} %reduce_sum.303, f32[32]{0:T(128)S(1)} %reduce_sum.300), channel_id=1, replica_groups=mesh['rows'=4,'segment'=4,'tm'=2] {'rows'}, use_global_device_ids=true, to_apply=%region_47.48 | all-reduce | flops 64 | bytes 512 | tf_op jit(solution)/shard_map/psum | solution.py:33
  299.0 3.6 %collective-permute-start.25 = (bf16[6,1,128,128]{3,2,1,0:T(8,128)(2,1)S(1)}, bf16[6,1,128,128]{3,2,1,0:T(8,128)(2,1)S(1)}, u32[]{:S(2)}, u32[]{:S(2)}) collective-permute-start(bf16[6,1,128,128]{3,2,1,0:T(8,128)(2,1)S(1)} %get-tuple-element.42), channel_id=1, source_target_pairs={{0,8},{8,16},{16,24},{1,9},{9,17},{17,25},{2,10},{10,18},{18,26},{... | collective-permute-start | bytes 589832 | tf_op jit(solution)/shard_map/ppermute | solution.py:21
  302.6 1.6 collective-permute-start.26
  304.2 3.1 collective-permute-done.25
  307.3 4.1 %collective-permute-done.26 = bf16[6,1,128,128]{3,2,1,0:T(8,128)(2,1)S(1)} collective-permute-done((bf16[6,1,128,128]{3,2,1,0:T(8,128)(2,1)S(1)}, bf16[6,1,128,128]{3,2,1,0:T(8,128)(2,1)S(1)}, u32[]{:S(2)}, u32[]{:S(2)}) %collective-permute-start.26) | collective-permute-done | bytes 196640 | tf_op jit(solution)/shard_map/ppermute | solution.py:24
  312.5 3.3 %convolution_select_fusion = f32[4,2,8,17,128]{4,2,3,1,0:T(8,128)S(1)} fusion(bf16[6,4,1,7,2,128]{5,3,4,1,0,2:T(8,128)(2,1)S(1)} %slice.302, bf16[6,4,1,8,17,128]{5,3,4,1,0,2:T(8,128)(2,1)S(1)} %copy.97, bf16[8,3,3,3,128,128]{5,4,3,2,1,0:T(8,128)(2,1)} %constant_dynamic-update-slice_fusion, s32[]{:T(128)S(6)} %add.269, pred[8,17]{0,1:T(8,128)(4,1)S(1)} %copy-done.13), kind=kOutput, calls=%fused_computation.12 | convolution fusion | flops 965533696 | bytes 2363532 | tf_op jit(solution)/shard_map/conv_general_dilated | solution.py:52
  (221 shorter events, 58.9 us)
Async XLA Ops:
  6.5 99.0 %all-gather.2.cloned.1.call-start = ((), (), s32[]{:S(2)}) async-start(), calls=%async_computation | async-start | bytes 4423680 | tf_op jit(solution)/shard_map/all_gather | solution.py:78
  7.3 32.4 %collective-permute-start.6 = (bf16[1,3,3,3,128,128]{5,4,3,2,1,0:T(8,128)(2,1)}, bf16[1,3,3,3,128,128]{5,4,3,2,1,0:T(8,128)(2,1)S(1)}, u32[]{:S(2)}, u32[]{:S(2)}) collective-permute-start(bf16[1,3,3,3,128,128]{5,4,3,2,1,0:T(8,128)(2,1)} %param.9), channel_id=1, source_target_pairs={{0,2},{2,4},{4,6},{6,0},{1,3},{3,5},{5,7},{7,1},{8,10},{10,12},{12... | collective-permute-start | bytes 2654216 | tf_op jit(solution)/shard_map/ppermute | solution.py:81
  39.6 39.8 %collective-permute-start.7 = (bf16[1,3,3,3,128,128]{5,4,3,2,1,0:T(8,128)(2,1)S(1)}, bf16[1,3,3,3,128,128]{5,4,3,2,1,0:T(8,128)(2,1)S(1)}, u32[]{:S(2)}, u32[]{:S(2)}) collective-permute-start(bf16[1,3,3,3,128,128]{5,4,3,2,1,0:T(8,128)(2,1)S(1)} %collective-permute-done.6), channel_id=1, source_target_pairs={{0,2},{2,4},{4,6},{6,0},{1,3},{3,5},{5,7},{7,1},{8,10},{10,12},{12... | collective-permute-start | bytes 2654216 | tf_op jit(solution)/shard_map/ppermute | solution.py:81
  79.5 21.1 %collective-permute-start.8 = (bf16[1,3,3,3,128,128]{5,4,3,2,1,0:T(8,128)(2,1)S(1)}, bf16[1,3,3,3,128,128]{5,4,3,2,1,0:T(8,128)(2,1)S(1)}, u32[]{:S(2)}, u32[]{:S(2)}) collective-permute-start(bf16[1,3,3,3,128,128]{5,4,3,2,1,0:T(8,128)(2,1)S(1)} %collective-permute-done.7), channel_id=1, source_target_pairs={{0,2},{2,4},{4,6},{6,0},{1,3},{3,5},{5,7},{7,1},{8,10},{10,12},{12... | collective-permute-start | bytes 2654216 | tf_op jit(solution)/shard_map/ppermute | solution.py:81
  83.2 2.3 collective-permute-start
  86.2 8.6 %collective-permute-start.1 = (bf16[6,1,128,128]{3,2,1,0:T(8,128)(2,1)}, bf16[6,1,128,128]{3,2,1,0:T(8,128)(2,1)S(1)}, u32[]{:S(2)}, u32[]{:S(2)}) collective-permute-start(bf16[6,1,128,128]{3,2,1,0:T(8,128)(2,1)} %get-tuple-element.56), channel_id=1, source_target_pairs={{0,8},{8,16},{16,24},{1,9},{9,17},{17,25},{2,10},{10,18},{18,26},{... | collective-permute-start | bytes 589832 | tf_op jit(solution)/shard_map/ppermute | solution.py:21
  89.9 9.0 %collective-permute-start.2 = (bf16[6,1,128,128]{3,2,1,0:T(8,128)(2,1)}, bf16[6,1,128,128]{3,2,1,0:T(8,128)(2,1)S(1)}, u32[]{:S(2)}, u32[]{:S(2)}) collective-permute-start(bf16[6,1,128,128]{3,2,1,0:T(8,128)(2,1)} %get-tuple-element.57), channel_id=1, source_target_pairs={{8,0},{16,8},{24,16},{9,1},{17,9},{25,17},{10,2},{18,10},{26,18},{... | collective-permute-start | bytes 589832 | tf_op jit(solution)/shard_map/ppermute | solution.py:24
  99.9 2.8 copy-start.2
  101.6 2.0 copy-start
  105.6 15.1 %copy-start.11 = (f32[128]{0:T(128)S(1)}, f32[128]{0:T(128)}, u32[]{:S(2)}) copy-start(f32[128]{0:T(128)} %get-tuple-element.70) | copy-start | bytes 1540
  105.6 15.1 %copy-start.12 = (f32[128]{0:T(128)S(1)}, f32[128]{0:T(128)}, u32[]{:S(2)}) copy-start(f32[128]{0:T(128)} %get-tuple-element.71) | copy-start | bytes 1540
  120.9 2.3 collective-permute-start.3
  123.3 7.1 %collective-permute-start.4 = (bf16[6,1,128,128]{3,2,1,0:T(8,128)(2,1)S(1)}, bf16[6,1,128,128]{3,2,1,0:T(8,128)(2,1)S(1)}, u32[]{:S(2)}, u32[]{:S(2)}) collective-permute-start(bf16[6,1,128,128]{3,2,1,0:T(8,128)(2,1)S(1)} %get-tuple-element.54), channel_id=1, source_target_pairs={{0,8},{8,16},{16,24},{1,9},{9,17},{17,25},{2,10},{10,18},{18,26},{... | collective-permute-start | bytes 589832 | tf_op jit(solution)/shard_map/ppermute | solution.py:21
  125.7 8.8 %collective-permute-start.5 = (bf16[6,1,128,128]{3,2,1,0:T(8,128)(2,1)S(1)}, bf16[6,1,128,128]{3,2,1,0:T(8,128)(2,1)S(1)}, u32[]{:S(2)}, u32[]{:S(2)}) collective-permute-start(bf16[6,1,128,128]{3,2,1,0:T(8,128)(2,1)S(1)} %get-tuple-element.55), channel_id=1, source_target_pairs={{8,0},{16,8},{24,16},{9,1},{17,9},{25,17},{10,2},{18,10},{26,18},{... | collective-permute-start | bytes 589832 | tf_op jit(solution)/shard_map/ppermute | solution.py:24
  135.0 0.7 copy-start.13
  139.0 1.2 copy-start.1
  139.0 10.9 %copy-start.3 = (f32[128]{0:T(128)S(1)}, f32[128]{0:T(128)}, u32[]{:S(2)}) copy-start(f32[128]{0:T(128)} %get-tuple-element.68) | copy-start | bytes 1540
  139.0 10.9 %copy-start.4 = (f32[128]{0:T(128)S(1)}, f32[128]{0:T(128)}, u32[]{:S(2)}) copy-start(f32[128]{0:T(128)} %get-tuple-element.69) | copy-start | bytes 1540
  150.2 2.3 collective-permute-start.9
  152.5 8.3 %collective-permute-start.10 = (bf16[6,1,128,128]{3,2,1,0:T(8,128)(2,1)S(1)}, bf16[6,1,128,128]{3,2,1,0:T(8,128)(2,1)S(1)}, u32[]{:S(2)}, u32[]{:S(2)}) collective-permute-start(bf16[6,1,128,128]{3,2,1,0:T(8,128)(2,1)S(1)} %get-tuple-element.52), channel_id=1, source_target_pairs={{0,8},{8,16},{16,24},{1,9},{9,17},{17,25},{2,10},{10,18},{18,26},{... | collective-permute-start | bytes 589832 | tf_op jit(solution)/shard_map/ppermute | solution.py:21
  156.1 8.8 %collective-permute-start.11 = (bf16[6,1,128,128]{3,2,1,0:T(8,128)(2,1)S(1)}, bf16[6,1,128,128]{3,2,1,0:T(8,128)(2,1)S(1)}, u32[]{:S(2)}, u32[]{:S(2)}) collective-permute-start(bf16[6,1,128,128]{3,2,1,0:T(8,128)(2,1)S(1)} %get-tuple-element.53), channel_id=1, source_target_pairs={{8,0},{16,8},{24,16},{9,1},{17,9},{25,17},{10,2},{18,10},{26,18},{... | collective-permute-start | bytes 589832 | tf_op jit(solution)/shard_map/ppermute | solution.py:24
  165.9 13.2 %copy-start.9 = (f32[128]{0:T(128)S(1)}, f32[128]{0:T(128)}, u32[]{:S(2)}) copy-start(f32[128]{0:T(128)} %get-tuple-element.66) | copy-start | bytes 1540
  165.9 13.2 %copy-start.10 = (f32[128]{0:T(128)S(1)}, f32[128]{0:T(128)}, u32[]{:S(2)}) copy-start(f32[128]{0:T(128)} %get-tuple-element.67) | copy-start | bytes 1540
  179.4 2.3 collective-permute-start.12
  181.7 8.3 %collective-permute-start.13 = (bf16[6,1,128,128]{3,2,1,0:T(8,128)(2,1)S(1)}, bf16[6,1,128,128]{3,2,1,0:T(8,128)(2,1)S(1)}, u32[]{:S(2)}, u32[]{:S(2)}) collective-permute-start(bf16[6,1,128,128]{3,2,1,0:T(8,128)(2,1)S(1)} %get-tuple-element.50), channel_id=1, source_target_pairs={{0,8},{8,16},{16,24},{1,9},{9,17},{17,25},{2,10},{10,18},{18,26},{... | collective-permute-start | bytes 589832 | tf_op jit(solution)/shard_map/ppermute | solution.py:21
  185.3 8.8 %collective-permute-start.14 = (bf16[6,1,128,128]{3,2,1,0:T(8,128)(2,1)S(1)}, bf16[6,1,128,128]{3,2,1,0:T(8,128)(2,1)S(1)}, u32[]{:S(2)}, u32[]{:S(2)}) collective-permute-start(bf16[6,1,128,128]{3,2,1,0:T(8,128)(2,1)S(1)} %get-tuple-element.51), channel_id=1, source_target_pairs={{8,0},{16,8},{24,16},{9,1},{17,9},{25,17},{10,2},{18,10},{26,18},{... | collective-permute-start | bytes 589832 | tf_op jit(solution)/shard_map/ppermute | solution.py:24
  208.7 2.3 collective-permute-start.15
  211.0 8.3 %collective-permute-start.16 = (bf16[6,1,128,128]{3,2,1,0:T(8,128)(2,1)S(1)}, bf16[6,1,128,128]{3,2,1,0:T(8,128)(2,1)S(1)}, u32[]{:S(2)}, u32[]{:S(2)}) collective-permute-start(bf16[6,1,128,128]{3,2,1,0:T(8,128)(2,1)S(1)} %get-tuple-element.48), channel_id=1, source_target_pairs={{0,8},{8,16},{16,24},{1,9},{9,17},{17,25},{2,10},{10,18},{18,26},{... | collective-permute-start | bytes 589832 | tf_op jit(solution)/shard_map/ppermute | solution.py:21
  214.6 8.8 %collective-permute-start.17 = (bf16[6,1,128,128]{3,2,1,0:T(8,128)(2,1)S(1)}, bf16[6,1,128,128]{3,2,1,0:T(8,128)(2,1)S(1)}, u32[]{:S(2)}, u32[]{:S(2)}) collective-permute-start(bf16[6,1,128,128]{3,2,1,0:T(8,128)(2,1)S(1)} %get-tuple-element.49), channel_id=1, source_target_pairs={{8,0},{16,8},{24,16},{9,1},{17,9},{25,17},{10,2},{18,10},{26,18},{... | collective-permute-start | bytes 589832 | tf_op jit(solution)/shard_map/ppermute | solution.py:24
  224.4 13.5 %copy-start.7 = (f32[128]{0:T(128)S(1)}, f32[128]{0:T(128)}, u32[]{:S(2)}) copy-start(f32[128]{0:T(128)} %get-tuple-element.62) | copy-start | bytes 1540
  224.5 13.5 %copy-start.8 = (f32[128]{0:T(128)S(1)}, f32[128]{0:T(128)}, u32[]{:S(2)}) copy-start(f32[128]{0:T(128)} %get-tuple-element.63) | copy-start | bytes 1540
  238.2 2.3 collective-permute-start.18
  240.5 8.3 %collective-permute-start.19 = (bf16[6,1,128,128]{3,2,1,0:T(8,128)(2,1)S(1)}, bf16[6,1,128,128]{3,2,1,0:T(8,128)(2,1)S(1)}, u32[]{:S(2)}, u32[]{:S(2)}) collective-permute-start(bf16[6,1,128,128]{3,2,1,0:T(8,128)(2,1)S(1)} %get-tuple-element.46), channel_id=1, source_target_pairs={{0,8},{8,16},{16,24},{1,9},{9,17},{17,25},{2,10},{10,18},{18,26},{... | collective-permute-start | bytes 589832 | tf_op jit(solution)/shard_map/ppermute | solution.py:21
  244.1 8.8 %collective-permute-start.20 = (bf16[6,1,128,128]{3,2,1,0:T(8,128)(2,1)S(1)}, bf16[6,1,128,128]{3,2,1,0:T(8,128)(2,1)S(1)}, u32[]{:S(2)}, u32[]{:S(2)}) collective-permute-start(bf16[6,1,128,128]{3,2,1,0:T(8,128)(2,1)S(1)} %get-tuple-element.47), channel_id=1, source_target_pairs={{8,0},{16,8},{24,16},{9,1},{17,9},{25,17},{10,2},{18,10},{26,18},{... | collective-permute-start | bytes 589832 | tf_op jit(solution)/shard_map/ppermute | solution.py:24
  267.5 2.3 collective-permute-start.21
  269.8 8.3 %collective-permute-start.22 = (bf16[6,1,128,128]{3,2,1,0:T(8,128)(2,1)S(1)}, bf16[6,1,128,128]{3,2,1,0:T(8,128)(2,1)S(1)}, u32[]{:S(2)}, u32[]{:S(2)}) collective-permute-start(bf16[6,1,128,128]{3,2,1,0:T(8,128)(2,1)S(1)} %get-tuple-element.44), channel_id=1, source_target_pairs={{0,8},{8,16},{16,24},{1,9},{9,17},{17,25},{2,10},{10,18},{18,26},{... | collective-permute-start | bytes 589832 | tf_op jit(solution)/shard_map/ppermute | solution.py:21
  273.4 8.8 %collective-permute-start.23 = (bf16[6,1,128,128]{3,2,1,0:T(8,128)(2,1)S(1)}, bf16[6,1,128,128]{3,2,1,0:T(8,128)(2,1)S(1)}, u32[]{:S(2)}, u32[]{:S(2)}) collective-permute-start(bf16[6,1,128,128]{3,2,1,0:T(8,128)(2,1)S(1)} %get-tuple-element.45), channel_id=1, source_target_pairs={{8,0},{16,8},{24,16},{9,1},{17,9},{25,17},{10,2},{18,10},{26,18},{... | collective-permute-start | bytes 589832 | tf_op jit(solution)/shard_map/ppermute | solution.py:24
  283.2 13.2 %copy-start.5 = (f32[128]{0:T(128)S(1)}, f32[128]{0:T(128)}, u32[]{:S(2)}) copy-start(f32[128]{0:T(128)} %get-tuple-element.58) | copy-start | bytes 1540
  283.2 13.2 %copy-start.6 = (f32[128]{0:T(128)S(1)}, f32[128]{0:T(128)}, u32[]{:S(2)}) copy-start(f32[128]{0:T(128)} %get-tuple-element.59) | copy-start | bytes 1540
  296.7 2.3 collective-permute-start.24
  299.0 8.3 %collective-permute-start.25 = (bf16[6,1,128,128]{3,2,1,0:T(8,128)(2,1)S(1)}, bf16[6,1,128,128]{3,2,1,0:T(8,128)(2,1)S(1)}, u32[]{:S(2)}, u32[]{:S(2)}) collective-permute-start(bf16[6,1,128,128]{3,2,1,0:T(8,128)(2,1)S(1)} %get-tuple-element.42), channel_id=1, source_target_pairs={{0,8},{8,16},{16,24},{1,9},{9,17},{17,25},{2,10},{10,18},{18,26},{... | collective-permute-start | bytes 589832 | tf_op jit(solution)/shard_map/ppermute | solution.py:21
  302.6 8.8 %collective-permute-start.26 = (bf16[6,1,128,128]{3,2,1,0:T(8,128)(2,1)S(1)}, bf16[6,1,128,128]{3,2,1,0:T(8,128)(2,1)S(1)}, u32[]{:S(2)}, u32[]{:S(2)}) collective-permute-start(bf16[6,1,128,128]{3,2,1,0:T(8,128)(2,1)S(1)} %get-tuple-element.43), channel_id=1, source_target_pairs={{8,0},{16,8},{24,16},{9,1},{17,9},{25,17},{10,2},{18,10},{26,18},{... | collective-permute-start | bytes 589832 | tf_op jit(solution)/shard_map/ppermute | solution.py:24
Sparse Core Ops, SparseCore 0:
  9.2 74.2 all-gather.1
